TPU v7x, 32 devices: a whole 2x2x4 slice. The times are simulated.
32 devices in a mesh: series: 8 (over z, y), tm: 4 (over x, core).
Axes of the slice: x: 2, y: 2, z: 4, core: 2. Of those that a mesh axis runs over, the one named last changes fastest.
Arguments:
- target: float32 [8, 16384], P('tm', 'series'), may hold values from -14 to 14
- location: float32 [8, 16384], P('tm', 'series'), may hold values from -6 to 6
- variance: float32 [8, 16384], P('tm', 'series'), may hold values from 0.25 to 4
- factor_drift: bfloat16 [8, 64, 16384], P('tm', None, 'series'), may hold values from -0.0234375 to 0.0234375
- loading: bfloat16 [64, 16384], P(None, ('series', 'tm'))
- node_ids: int32 [3, 16384], P(None, 'series'), may hold values from 0 to 2047, as said below
- level_weight: float32 [4, 8], P(None, 'tm'), may hold values from 0.5 to 2
Outputs:
- gradient_location: float32 [8, 16384], P('tm', 'series')
- gradient_variance: float32 [8, 16384], P('tm', 'series')
- gradient_drift: float32 [8, 64, 16384], P('tm', None, 'series')
- gradient_loading: float32 [64, 16384], P(None, ('series', 'tm'))
Inputs may be any that keep to these rules, and one draw needn't show every extreme that they name: `node_ids`: at each upper level node numbers never fall along the series, begin at 0 and rise by at most one from a series to the next; every node of a level is a union of whole nodes of the level below; a level-one node holds 5 series or more; every level-two node but the last holds 64 level-one nodes or more (one at least), every level-three node but the last 4 level-two nodes or more; level one has exactly 2048 nodes.
All inputs are finite; a program needn't handle non-finite values.
Results may differ from a plain program's by a relative error of at most 0.0003.
Values may be sent and summed in bfloat16 or wider, within the bound.
A program may use at most 64 MiB of HBM per device.

v0:
```python
import jax
import jax.numpy as jnp
from jax import lax
from jax.sharding import PartitionSpec as P

highest = lax.Precision.HIGHEST


def entering(value, axis, combine, identity, reverse):
    length, here = (lax.axis_size(axis), lax.axis_index(axis))
    everything = jax.tree.map(lambda part: lax.all_gather(part, axis), value)
    start = jax.tree.map(
        lambda part, zero: jnp.broadcast_to(jnp.asarray(zero, part.dtype), part.shape),
        value,
        identity,
    )

    def hop(k, before):
        at = length - 1 - k if reverse else k
        reached = at > here if reverse else at < here
        new = combine(before, jax.tree.map(lambda part: part[at], everything))
        return jax.tree.map(lambda a, b: jnp.where(reached, a, b), new, before)

    return lax.fori_loop(0, length, hop, start)


def node_terms(vectors, variance, residual, owned):
    safe_variance = jnp.where(variance > 0.0, variance, 1.0)
    weights = 1.0 / safe_variance
    scaled = vectors * (weights * owned)[:, None, :]
    capacity_part = jnp.einsum("trn,tkn->trk", scaled, vectors, precision=highest)
    projection = jnp.einsum("trn,tn->tr", scaled, residual, precision=highest)
    return (capacity_part, projection, weights)


def level_solve(capacity_sum, projection_sum):
    order_size = capacity_sum.shape[-1]
    identity = jnp.eye(order_size, dtype=jnp.float32)
    capacitance = identity + capacity_sum
    lower_factors = jnp.linalg.cholesky(capacitance)
    inverse = jax.vmap(
        lambda lower_factor: jax.scipy.linalg.cho_solve((lower_factor, True), identity)
    )(lower_factors)
    coefficient = jnp.einsum("trk,tk->tr", inverse, projection_sum, precision=highest)
    return (inverse, coefficient)


def node_grads(vectors, weights, residual, inverse, coefficient):
    solved = jnp.einsum("trk,tkn->trn", inverse, vectors, precision=highest)
    fitted = jnp.einsum("trn,tr->tn", vectors, coefficient, precision=highest)
    whitened = weights * (residual - fitted)
    leverage = jnp.sum(vectors * solved, axis=1)
    variance_grad = 0.5 * (weights - weights * weights * leverage - whitened * whitened)
    factor_grad = solved * weights[:, None, :] - coefficient[:, :, None] * whitened[:, None, :]
    return (-whitened, variance_grad, factor_grad)


def join_forward(earlier, latter):
    latter_empty = latter[4] < 0.0
    earlier_empty = earlier[3] < 0.0
    extend = (latter[3] == latter[4]) & (earlier[4] == latter[3])
    carried = jnp.where(latter_empty | extend, 1.0, 0.0).astype(jnp.float32)
    return (
        latter[0] + carried[:, None, None] * earlier[0],
        latter[1] + carried[:, None] * earlier[1],
        latter[2] + carried[:, None] * earlier[2],
        jnp.where(earlier_empty, latter[3], earlier[3]),
        jnp.where(latter_empty, earlier[4], latter[4]),
    )


def join_backward(earlier, latter):
    latter_empty = latter[3] < 0.0
    earlier_empty = earlier[3] < 0.0
    extend = (latter[3] == latter[4]) & (latter[4] == earlier[3])
    carried = jnp.where(latter_empty | extend, 1.0, 0.0).astype(jnp.float32)
    return (
        latter[0] + carried[:, None, None] * earlier[0],
        latter[1] + carried[:, None] * earlier[1],
        latter[2] + carried[:, None] * earlier[2],
        jnp.where(latter_empty, earlier[3], latter[3]),
        jnp.where(earlier_empty, latter[4], earlier[4]),
    )


def level_nodes(packed, member_ids, slot_total, step_count, factor_size):
    summed = jax.ops.segment_sum(
        packed, member_ids, num_segments=slot_total, indices_are_sorted=True
    )
    width = step_count * factor_size
    node_vectors = jnp.transpose(
        summed[:, :width].reshape(slot_total, step_count, factor_size), (1, 2, 0)
    )
    node_variance = summed[:, width : width + step_count].T
    node_residual = summed[:, width + step_count :].T
    return (node_vectors, node_variance, node_residual)


def local(target, location, variance, factor_drift, loading, node_ids, level_weight):
    full_loading = lax.all_gather(loading, "tm", axis=1, tiled=True)
    vectors = full_loading.astype(jnp.float32)[None] + factor_drift.astype(jnp.float32)
    residual = target - location
    step_count, factor_size, series_count = vectors.shape
    upper_count = node_ids.shape[0]
    bottom_cap, bottom_proj, bottom_weights = node_terms(
        vectors, variance, residual, jnp.ones((series_count,), jnp.float32)
    )
    bottom_cap, bottom_proj = lax.psum((bottom_cap, bottom_proj), "series")
    local_ids = node_ids - node_ids[:, :1]
    packed = jnp.concatenate(
        [
            jnp.transpose(vectors, (2, 0, 1)).reshape(series_count, step_count * factor_size),
            variance.T,
            residual.T,
        ],
        axis=1,
    )
    slot_sizes = [series_count // 4] + [16] * (upper_count - 1)
    last_slot = local_ids[:, -1]
    grouped = []
    first_parts = ([], [], [])
    last_parts = ([], [], [])
    for level_index in range(upper_count):
        node_vectors, node_variance, node_residual = level_nodes(
            packed, local_ids[level_index], slot_sizes[level_index], step_count, factor_size
        )
        grouped.append((node_vectors, node_variance, node_residual))
        final = last_slot[level_index]
        first_parts[0].append(node_vectors[..., 0])
        first_parts[1].append(node_variance[..., 0])
        first_parts[2].append(node_residual[..., 0])
        last_parts[0].append(lax.dynamic_index_in_dim(node_vectors, final, 2, keepdims=False))
        last_parts[1].append(lax.dynamic_index_in_dim(node_variance, final, 1, keepdims=False))
        last_parts[2].append(lax.dynamic_index_in_dim(node_residual, final, 1, keepdims=False))
    first_vectors = jnp.stack(first_parts[0])
    first_variance = jnp.stack(first_parts[1])
    first_residual = jnp.stack(first_parts[2])
    last_vectors = jnp.stack(last_parts[0])
    last_variance = jnp.stack(last_parts[1])
    last_residual = jnp.stack(last_parts[2])
    first_id = node_ids[:, 0].astype(jnp.float32)
    last_id = node_ids[:, -1].astype(jnp.float32)
    start_empty = (
        jnp.zeros_like(first_vectors),
        jnp.zeros_like(first_variance),
        jnp.zeros_like(first_residual),
        jnp.full((upper_count,), -1.0, jnp.float32),
        jnp.full((upper_count,), -1.0, jnp.float32),
    )
    before = entering(
        (last_vectors, last_variance, last_residual, first_id, last_id),
        "series",
        join_forward,
        start_empty,
        False,
    )
    after = entering(
        (first_vectors, first_variance, first_residual, first_id, last_id),
        "series",
        join_backward,
        start_empty,
        True,
    )
    left_gate = (before[4] == first_id).astype(jnp.float32)
    right_gate = (after[3] == last_id).astype(jnp.float32)
    left_vectors = before[0] * left_gate[:, None, None]
    left_variance = before[1] * left_gate[:, None]
    left_residual = before[2] * left_gate[:, None]
    right_vectors = after[0] * right_gate[:, None, None]
    right_variance = after[1] * right_gate[:, None]
    right_residual = after[2] * right_gate[:, None]
    full_nodes = []
    upper_caps = []
    upper_projs = []
    upper_weights = []
    for level_index in range(upper_count):
        node_vectors, node_variance, node_residual = grouped[level_index]
        final = last_slot[level_index]
        node_vectors = (
            node_vectors.at[:, :, 0]
            .add(left_vectors[level_index])
            .at[:, :, final]
            .add(right_vectors[level_index])
        )
        node_variance = (
            node_variance.at[:, 0]
            .add(left_variance[level_index])
            .at[:, final]
            .add(right_variance[level_index])
        )
        node_residual = (
            node_residual.at[:, 0]
            .add(left_residual[level_index])
            .at[:, final]
            .add(right_residual[level_index])
        )
        slot_order = jnp.arange(slot_sizes[level_index], dtype=jnp.int32)
        owned = 1.0 - right_gate[level_index] * (slot_order == final).astype(jnp.float32)
        capacity_part, projection, weights = node_terms(
            node_vectors, node_variance, node_residual, owned
        )
        full_nodes.append((node_vectors, node_residual))
        upper_caps.append(capacity_part)
        upper_projs.append(projection)
        upper_weights.append(weights)
    upper_cap = jnp.stack(upper_caps)
    upper_proj = jnp.stack(upper_projs)
    upper_cap, upper_proj = lax.psum((upper_cap, upper_proj), "series")
    cap_sums = jnp.concatenate([bottom_cap[None], upper_cap], axis=0)
    proj_sums = jnp.concatenate([bottom_proj[None], upper_proj], axis=0)
    inverse, coefficient = level_solve(cap_sums[0], proj_sums[0])
    location_grad, variance_grad, factor_grad = node_grads(
        vectors, bottom_weights, residual, inverse, coefficient
    )
    total_location = level_weight[0][:, None] * location_grad
    total_variance = level_weight[0][:, None] * variance_grad
    total_factor = level_weight[0][:, None, None] * factor_grad
    for level_index in range(upper_count):
        inverse, coefficient = level_solve(cap_sums[level_index + 1], proj_sums[level_index + 1])
        node_vectors, node_residual = full_nodes[level_index]
        node_location, node_variance, node_factor = node_grads(
            node_vectors, upper_weights[level_index], node_residual, inverse, coefficient
        )
        member_ids = local_ids[level_index]
        weight_now = level_weight[level_index + 1]
        total_location = total_location + weight_now[:, None] * jnp.take(
            node_location, member_ids, axis=1
        )
        total_variance = total_variance + weight_now[:, None] * jnp.take(
            node_variance, member_ids, axis=1
        )
        total_factor = total_factor + weight_now[:, None, None] * jnp.take(
            node_factor, member_ids, axis=2
        )
    loading_total = lax.psum_scatter(
        jnp.sum(total_factor, axis=0), "tm", scatter_dimension=1, tiled=True
    )
    return (total_location, total_variance, total_factor, loading_total)


def solution(mesh):
    return jax.shard_map(
        local,
        mesh=mesh,
        in_specs=(
            P("tm", "series"),
            P("tm", "series"),
            P("tm", "series"),
            P("tm", None, "series"),
            P(None, ("series", "tm")),
            P(None, "series"),
            P(None, "tm"),
        ),
        out_specs=(
            P("tm", "series"),
            P("tm", "series"),
            P("tm", None, "series"),
            P(None, ("series", "tm")),
        ),
        check_vma=False,
    )
```

profile of v0, /device:TPU:1, one launch (start us, length us, event | category | flops | bytes accessed | tf_op | source)
XLA Modules:
  0.0 499.9 jit_solution(12526921175785902977)
XLA Ops:
  7.2 0.8 slice_reduce_fusion.1
  8.0 0.8 broadcast_subtract_fusion
  12.0 7.3 %all_gather.51 = bf16[64,2048]{1,0:T(8,128)(2,1)S(1)} all-gather(bf16[64,512]{1,0:T(8,128)(2,1)} %param.60), channel_id=1, replica_groups=mesh['series'=8,'tm'=4] {'tm'}, dimensions={1}, use_global_device_ids=true | all-gather | bytes 327680 | tf_op jit(solution)/shard_map/all_gather | solution.py:100
  19.4 1.2 convert_add_fusion
  21.3 1.3 copy.416
  22.7 15.6 %scatter_custom_fusion.1 = f32[16,132]{1,0:T(8,128)S(1)} fusion(s32[2048]{0:T(1024)S(1)} %bitcast.406, f32[]{:T(128)} %constant.605.clone.1, f32[2048,2]{1,0:T(8,128)S(1)} %copy.417, f32[2048,2]{1,0:T(8,128)} %copy.416, f32[2048,128]{1,0:T(8,128)S(1)} %copy.415), kind=kCustom, calls=%fused_computation.173 | custom fusion | flops 811008 | bytes 2121988 | tf_op jit(solution)/shard_map/scatter-add | solution.py:87
  38.3 15.6 %scatter_custom_fusion.2 = f32[16,132]{1,0:T(8,128)S(1)} fusion(s32[2048]{0:T(1024)S(1)} %bitcast.403, f32[]{:T(128)} %constant.605.clone.1, f32[2048,2]{1,0:T(8,128)S(1)} %copy.417, f32[2048,2]{1,0:T(8,128)} %copy.416, f32[2048,128]{1,0:T(8,128)S(1)} %copy.415), kind=kCustom, calls=%fused_computation.171 | custom fusion | flops 811008 | bytes 2121988 | tf_op jit(solution)/shard_map/scatter-add | solution.py:87
  54.0 14.5 %scatter_custom_fusion = f32[512,132]{1,0:T(8,128)S(1)} fusion(s32[2048]{0:T(1024)S(1)} %bitcast.400, f32[]{:T(128)} %constant.605.clone.1, f32[2048,2]{1,0:T(8,128)S(1)} %copy.417, f32[2048,2]{1,0:T(8,128)} %copy.416, f32[2048,128]{1,0:T(8,128)S(1)} %copy.415), kind=kCustom, calls=%fused_computation.78 | custom fusion | flops 811008 | bytes 2383876 | tf_op jit(solution)/shard_map/scatter-add | solution.py:87
  68.7 0.9 convert_reduce_fusion
  74.5 17.1 %all-gather.9 = f32[8,3,2]{1,2,0:T(2,128)S(1)} all-gather(f32[1,3,2]{1,2,0:T(2,128)S(1)} %maximum_bitcast_fusion.1), channel_id=6, replica_groups=mesh['series'=8,'tm'=4] {'series'}, dimensions={0}, use_global_device_ids=true | all-gather | bytes 216 | tf_op jit(solution)/shard_map/all_gather | solution.py:11
  92.1 12.8 %all-gather.8 = f32[8,3,2]{1,2,0:T(2,128)S(1)} all-gather(f32[1,3,2]{1,2,0:T(2,128)S(1)} %maximum_bitcast_fusion), channel_id=5, replica_groups=mesh['series'=8,'tm'=4] {'series'}, dimensions={0}, use_global_device_ids=true | all-gather | bytes 216 | tf_op jit(solution)/shard_map/all_gather | solution.py:11
  105.2 24.0 %all-gather = f32[24,2,64]{2,1,0:T(2,128)S(1)} all-gather(f32[3,2,64]{2,1,0:T(2,128)S(1)} %pad_maximum_fusion.2), channel_id=2, replica_groups=mesh['series'=8,'tm'=4] {'series'}, dimensions={0}, use_global_device_ids=true | all-gather | bytes 13824 | tf_op jit(solution)/shard_map/all_gather | solution.py:11
  130.9 15.1 %all-reduce.3 = (f32[24]{0:T(128)S(1)}, f32[24]{0:T(128)S(1)}) all-reduce(f32[24]{0:T(128)S(1)} %dynamic-update-slice.56, f32[24]{0:T(128)S(1)} %dynamic-update-slice.57), channel_id=3, replica_groups=mesh['series'=8,'tm'=4] {'series'}, use_global_device_ids=true, to_apply=%add | all-reduce | flops 48 | bytes 384
  146.2 1.0 while.60
  147.6 12.9 %all-gather.11 = f32[8,3,2]{1,2,0:T(2,128)S(1)} all-gather(f32[1,3,2]{1,2,0:T(2,128)S(1)} %bitcast.439), channel_id=9, replica_groups=mesh['series'=8,'tm'=4] {'series'}, dimensions={0}, use_global_device_ids=true | all-gather | bytes 216 | tf_op jit(solution)/shard_map/all_gather | solution.py:11
  161.0 14.4 %all-gather.10 = f32[8,3,2]{1,2,0:T(2,128)S(1)} all-gather(f32[1,3,2]{1,2,0:T(2,128)S(1)} %bitcast.440), channel_id=8, replica_groups=mesh['series'=8,'tm'=4] {'series'}, dimensions={0}, use_global_device_ids=true | all-gather | bytes 216 | tf_op jit(solution)/shard_map/all_gather | solution.py:11
  175.5 24.1 %all-gather.5 = f32[24,2,64]{2,1,0:T(2,128)S(1)} all-gather(f32[3,2,64]{2,1,0:T(2,128)S(1)} %pad_maximum_fusion.3), channel_id=7, replica_groups=mesh['series'=8,'tm'=4] {'series'}, dimensions={0}, use_global_device_ids=true | all-gather | bytes 13824 | tf_op jit(solution)/shard_map/all_gather | solution.py:11
  199.7 1.0 while.61
  200.9 1.3 add_select_fusion.12
  202.9 0.7 and_reduce_fusion.5
  203.7 0.8 and_reduce_fusion
  204.5 1.9 add_select_fusion.11
  206.5 1.3 select_subtract_fusion
  208.6 0.8 and_reduce_fusion.3
  209.4 0.7 add_select_fusion
  210.6 1.2 fusion.110
  213.3 1.3 fusion.111
  217.0 1.3 add_select_fusion.10
  218.4 1.9 add_select_fusion.9
  221.4 1.3 fusion.22
  222.6 1.1 fusion.20
  223.8 27.0 %all-reduce.2 = (f32[2,64,64]{1,2,0:T(8,128)S(1)}, f32[3,2,64]{2,1,0:T(2,128)S(1)}, f32[2,64]{1,0:T(2,128)S(1)}) all-reduce(f32[2,64,64]{1,2,0:T(8,128)S(1)} %fusion.22, f32[3,2,64]{2,1,0:T(2,128)S(1)} %pad_maximum_fusion.4, f32[2,64]{1,0:T(2,128)S(1)} %bitcast.431), channel_id=1, replica_groups=mesh['series'=8,'tm'=4] {'series'}, use_global_device_ids=true, to_apply=%region_0.1 | all-reduce | flops 8704 | bytes 69632 | tf_op jit(solution)/shard_map/psum | solution.py:108
  251.6 61.2 %all-reduce.6.cloned.1.call-done = f32[3,2,64,64]{2,3,1,0:T(8,128)} async-done(((f32[3,2,64,64]{2,3,1,0:T(8,128)}), f32[3,2,64,64]{2,3,1,0:T(8,128)}) %all-reduce.6.cloned.1.call-update) | async-done | bytes 98320 | tf_op jit(solution)/shard_map/psum | solution.py:208
  312.8 0.9 fusion.42
  313.8 11.7 %custom-call.28 = f32[2,64,64]{2,1,0:T(8,128)S(1)} custom-call(f32[2,64,64]{2,1,0:T(8,128)S(1)} %fusion.48), custom_call_target="Cholesky" | custom-call | tf_op jit(solution)/shard_map/jit(cholesky)/cholesky | solution.py:40
  325.7 11.7 %custom-call.26 = f32[2,64,64]{2,1,0:T(8,128)S(1)} custom-call(f32[2,64,64]{2,1,0:T(8,128)S(1)} %fusion.53), custom_call_target="Cholesky" | custom-call | tf_op jit(solution)/shard_map/jit(cholesky)/cholesky | solution.py:40
  337.5 11.7 %custom-call.24 = f32[2,64,64]{2,1,0:T(8,128)S(1)} custom-call(f32[2,64,64]{2,1,0:T(8,128)S(1)} %fusion.58), custom_call_target="Cholesky" | custom-call | tf_op jit(solution)/shard_map/jit(cholesky)/cholesky | solution.py:40
  349.4 11.7 %custom-call.22 = f32[2,64,64]{2,1,0:T(8,128)S(1)} custom-call(f32[2,64,64]{2,1,0:T(8,128)S(1)} %fusion.63), custom_call_target="Cholesky" | custom-call | tf_op jit(solution)/shard_map/jit(cholesky)/cholesky | solution.py:40
  361.7 9.8 %custom-call.25 = f32[2,1,64,64]{2,3,1,0:T(8,128)S(1)} custom-call(f32[2,1,64,64]{3,2,1,0:T(8,128)S(1)} %get-tuple-element.899), custom_call_target="InvertDiagBlocksLowerTriangular" | custom-call | tf_op jit(solution)/shard_map/vmap(jit(_cho_solve))/triangular_solve | solution.py:42
  373.1 1.0 copy.486
  374.1 7.8 %gather_fusion = f32[2048,2,64]{2,1,0:T(2,128)S(1)} fusion(f32[2,64,512]{1,0,2:T(2,128)} %copy.486, s32[2048]{0:T(1024)S(1)} %broadcast_clamp_fusion), kind=kCustom, calls=%fused_computation.8 | custom fusion | bytes 2105344 | tf_op jit(solution)/shard_map/jit(_take)/gather | solution.py:232
  381.9 2.2 copy.487
  384.1 9.8 %custom-call.27 = f32[2,1,64,64]{2,3,1,0:T(8,128)S(1)} custom-call(f32[2,1,64,64]{3,2,1,0:T(8,128)S(1)} %get-tuple-element.898), custom_call_target="InvertDiagBlocksLowerTriangular" | custom-call | tf_op jit(solution)/shard_map/vmap(jit(_cho_solve))/triangular_solve | solution.py:42
  395.2 6.8 %gather_fusion.7 = f32[2048,2,64]{2,1,0:T(2,128)S(1)} fusion(f32[2,64,16]{1,0,2:T(2,128)S(1)} %copy.488, s32[2048]{0:T(1024)S(1)} %get-tuple-element.940), kind=kCustom, calls=%fused_computation.2.clone | custom fusion | bytes 2105344 | tf_op jit(solution)/shard_map/jit(_take)/gather | solution.py:232
  402.0 2.2 copy.489
  404.1 9.8 %custom-call.29 = f32[2,1,64,64]{2,3,1,0:T(8,128)S(1)} custom-call(f32[2,1,64,64]{3,2,1,0:T(8,128)S(1)} %get-tuple-element.900), custom_call_target="InvertDiagBlocksLowerTriangular" | custom-call | tf_op jit(solution)/shard_map/vmap(jit(_cho_solve))/triangular_solve | solution.py:42
  415.2 6.8 %gather_fusion.8 = f32[2048,2,64]{2,1,0:T(2,128)S(1)} fusion(f32[2,64,16]{1,0,2:T(2,128)S(1)} %copy.490, s32[2048]{0:T(1024)S(1)} %fusion.94), kind=kCustom, calls=%fused_computation.7.clone | custom fusion | bytes 2105344 | tf_op jit(solution)/shard_map/jit(_take)/gather | solution.py:232
  422.0 2.1 copy.491
  424.1 10.1 %custom-call.23 = f32[2,1,64,64]{2,3,1,0:T(8,128)S(1)} custom-call(f32[2,1,64,64]{3,2,1,0:T(8,128)S(1)} %get-tuple-element.897), custom_call_target="InvertDiagBlocksLowerTriangular" | custom-call | tf_op jit(solution)/shard_map/vmap(jit(_cho_solve))/triangular_solve | solution.py:42
  434.7 2.1 multiply_reduce_fusion
  437.0 0.7 fusion.27
  437.9 7.6 %gather_fusion.4 = f32[2048,2]{1,0:T(8,128)} fusion(f32[2,512]{0,1:T(8,128)S(1)} %copy.478, s32[2048]{0:T(1024)S(1)} %get-tuple-element.939), kind=kCustom, calls=%fused_computation.3.clone | custom fusion | bytes 40960 | tf_op jit(solution)/shard_map/jit(_take)/gather | solution.py:229
  445.6 1.6 copy.479
  447.2 7.6 %gather_fusion.5 = f32[2048,2]{1,0:T(8,128)} fusion(f32[2,16]{0,1:T(8,128)S(1)} %copy.481, s32[2048]{0:T(1024)S(1)} %get-tuple-element.940), kind=kCustom, calls=%fused_computation.5.clone | custom fusion | bytes 40960 | tf_op jit(solution)/shard_map/jit(_take)/gather | solution.py:229
  454.8 1.6 copy.482
  456.5 7.6 %gather_fusion.6 = f32[2048,2]{1,0:T(8,128)} fusion(f32[2,16]{0,1:T(8,128)S(1)} %copy.484, s32[2048]{0:T(1024)S(1)} %fusion.94), kind=kCustom, calls=%fused_computation.6.clone | custom fusion | bytes 40960 | tf_op jit(solution)/shard_map/jit(_take)/gather | solution.py:229
  464.1 1.6 copy.485
  465.7 0.7 fusion.76
  466.4 3.9 fusion.112
  470.5 5.5 %gather_fusion.1 = f32[2048,2]{1,0:T(8,128)S(1)} fusion(f32[2,512]{0,1:T(8,128)S(1)} %copy.466, s32[2048]{0:T(1024)S(1)} %get-tuple-element.939), kind=kCustom, calls=%fused_computation.clone | custom fusion | bytes 40960 | tf_op jit(solution)/shard_map/jit(_take)/gather | solution.py:226
  476.4 5.5 %gather_fusion.2 = f32[2048,2]{1,0:T(8,128)S(1)} fusion(f32[2,16]{0,1:T(8,128)S(1)} %copy.471, s32[2048]{0:T(1024)S(1)} %get-tuple-element.940), kind=kCustom, calls=%fused_computation.1.clone | custom fusion | bytes 40960 | tf_op jit(solution)/shard_map/jit(_take)/gather | solution.py:226
  482.3 5.5 %gather_fusion.3 = f32[2048,2]{1,0:T(8,128)S(1)} fusion(f32[2,16]{0,1:T(8,128)S(1)} %copy.476, s32[2048]{0:T(1024)S(1)} %fusion.94), kind=kCustom, calls=%fused_computation.4.clone | custom fusion | bytes 40960 | tf_op jit(solution)/shard_map/jit(_take)/gather | solution.py:226
  488.1 0.7 fusion.79
  488.8 4.3 reduce-scatter.2.cloned.1.call-done
  (259 shorter events, 23.6 us)
Async XLA Ops:
  7.2 305.6 %all-reduce.6.cloned.1.call-start = ((), (), s32[]{:S(2)}) async-start(), calls=%async_computation.1 | async-start | bytes 393216 | tf_op jit(solution)/shard_map/psum | solution.py:208
  19.4 1.5 copy-start.4
  19.4 1.5 copy-start.5
  20.6 0.8 copy-start.3
  68.5 60.7 %copy-start.10 = (u32[32]{0:T(128)S(1)}, u32[32]{0:T(128)}, u32[]{:S(2)}) copy-start(u32[32]{0:T(128)} %constant.627) | copy-start | bytes 388
  68.5 140.1 %copy-start.8 = (s32[3]{0:T(128)S(1)}, s32[3]{0:T(128)}, u32[]{:S(2)}) copy-start(s32[3]{0:T(128)} %constant.615.clone.1) | copy-start | bytes 40
  68.6 140.1 %copy-start.9 = (s32[3]{0:T(128)S(1)}, s32[3]{0:T(128)}, u32[]{:S(2)}) copy-start(s32[3]{0:T(128)} %constant.616.clone.1) | copy-start | bytes 40
  105.0 116.3 %copy-start = (bf16[2,64,2048]{2,1,0:T(8,128)(2,1)S(1)}, bf16[2,64,2048]{2,1,0:T(8,128)(2,1)}, u32[]{:S(2)}) copy-start(bf16[2,64,2048]{2,1,0:T(8,128)(2,1)} %param.59) | copy-start | bytes 1572868
  216.5 34.4 %copy-start.6 = (f32[4,2]{0,1:T(2,128)S(1)}, f32[4,2]{0,1:T(2,128)}, u32[]{:S(2)}) copy-start(f32[4,2]{0,1:T(2,128)} %param.62) | copy-start | bytes 100
  216.5 276.6 %reduce-scatter.2.cloned.1.call-start = ((), (), s32[]{:S(2)}) async-start(), calls=%async_computation.2 | async-start | bytes 655360 | tf_op jit(solution)/shard_map/reduce_scatter | solution.py:235
  437.7 27.9 %copy-start.7 = (f32[2]{0:T(128)S(1)}, f32[2]{0:T(128)}, u32[]{:S(2)}) copy-start(f32[2]{0:T(128)} %broadcast_multiply_fusion.9) | copy-start | bytes 28
  437.8 28.6 %copy-start.1 = (f32[2048,2,64]{0,2,1:T(8,128)S(1)}, f32[2048,2,64]{0,2,1:T(8,128)}, u32[]{:S(2)}) copy-start(f32[2048,2,64]{0,2,1:T(8,128)} %copy.487) | copy-start | bytes 3145732
  437.8 28.6 %copy-start.2 = (f32[2048,2,64]{0,2,1:T(8,128)S(1)}, f32[2048,2,64]{0,2,1:T(8,128)}, u32[]{:S(2)}) copy-start(f32[2048,2,64]{0,2,1:T(8,128)} %copy.489) | copy-start | bytes 3145732
Sparse Core Ops, SparseCore 0:
  216.6 96.1 all-reduce.5
  470.4 22.5 reduce-scatter.1
where the time goes:
time: 501 us; the launch traced here: 500 us
  other arithmetic  161 us (32%)
  blocking collectives  155 us (31%)
  local copies, waits for them, and re-layouts  85.6 us (17%)
  waiting for transfers between devices  65.5 us (13%)
  between operations  21.3 us (4%)
  matrix products  11.3 us (2%)
    all_gather x6, blocking collectives, entering(): everything = jax.tree.map(lambda part: lax.all_gather(part, axis), value)  105 us
    psum x1, waiting for transfers between devices, local(): upper_cap, upper_proj = lax.psum((upper_cap, upper_proj), 'series')  61.2 us
    another operation x10, other arithmetic, level_solve(): lower_factors = jnp.linalg.cholesky(capacitance)  47.4 us
    scatter-add x3, other arithmetic, level_nodes(): jax.ops.segment_sum(packed, member_ids, num_segments=slot_total, indices_...  45.7 us
    another operation x6, other arithmetic, level_solve(): jax.scipy.linalg.cho_solve((lower_factor, True), identity)  39.6 us
    gather x6, local copies, waits for them, and re-layouts, local(): jnp.take(node_factor, member_ids, axis=2)  27.8 us
    gather x6, local copies, waits for them, and re-layouts, local(): jnp.take(node_variance, member_ids, axis=1)  27.6 us
    psum x1, blocking collectives, local(): bottom_cap, bottom_proj = lax.psum((bottom_cap, bottom_proj), 'series')  27 us
  transfers between devices with their start and end apart: 2, of which 2 were waited for; matrix products, arithmetic and copies ran while one was open for 5% of the time, Pallas kernels for 0%

commit v1 on v0

v1 whole, which is shorter than its diff:
```python
import functools

import jax
import jax.numpy as jnp
from jax import lax
from jax.experimental import pallas as pl
from jax.experimental.pallas import tpu as pltpu
from jax.sharding import PartitionSpec as P

MESH = pl.DeviceIdType.MESH
F32 = jnp.float32
BF16 = jnp.bfloat16
SMALL = 16
NT = (((1,), (1,)), ((), ()))
NN = (((1,), (0,)), ((), ()))
TN = (((0,), (0,)), ((), ()))


def split(x):
    hi = x.astype(BF16)
    return hi, (x - hi.astype(F32)).astype(BF16)


def bdot(a, b, dims):
    return lax.dot_general(a, b, dims, preferred_element_type=F32)


def dot3(a, b, dims):
    ah, al = a
    bh, bl = b
    return bdot(ah, bh, dims) + (bdot(ah, bl, dims) + bdot(al, bh, dims))


def exact(a, b, dims):
    return lax.dot_general(
        a, b, dims, precision=lax.Precision.HIGHEST, preferred_element_type=F32
    )


def invert(a, size):
    lane = lax.broadcasted_iota(jnp.int32, a.shape, 1)
    row = lax.broadcasted_iota(jnp.int32, a.shape, 0)
    for k in range(size):
        pivot = 1.0 / a[k : k + 1, k : k + 1]
        col = a[:, k : k + 1]
        here = lane[:1] == k
        new_row = jnp.where(here, 1.0, a[k : k + 1, :]) * pivot
        rest = jnp.where(lane == k, 0.0, a) - col * new_row
        a = jnp.where(row == k, new_row, rest)
    return a


def kernel(
    n_series, n_tm,
    target_ref, location_ref, variance_ref, drift_ref, loading_ref, ids_ref, weight_ref,
    gloc_ref, gvar_ref, gdrift_ref, gload_ref,
    lbuf, x, hot, v, z, bnd, cs, crecv, invs, g, gs, lsend, lrecv,
    lsem_s, lsem_r, bsem_s, bsem_r, csem_s, csem_r, isem_s, isem_r, gsem_s, gsem_r,
):
    steps, rank, count = drift_ref.shape
    upper = ids_ref.shape[0]
    slots = hot.shape[0]
    wide = rank + 16
    mats = (upper + 1) * steps
    offsets = [0] + [slots - SMALL * (upper - 1 - i) for i in range(upper - 1)]
    part = count // n_tm
    me = lax.axis_index("series")
    mt = lax.axis_index("tm")

    barrier = pltpu.get_barrier_semaphore()

    def hello(k, c):
        pl.semaphore_signal(
            barrier, inc=1, device_id={"series": lax.rem(me + k, n_series)}, device_id_type=MESH
        )
        return c

    lax.fori_loop(1, n_series, hello, 0)
    for k in range(1, n_tm):
        pl.semaphore_signal(
            barrier, inc=1, device_id={"tm": lax.rem(mt + k, n_tm)}, device_id_type=MESH
        )
    pl.semaphore_wait(barrier, n_series - 1 + n_tm - 1)

    loads = []
    for k in range(1, n_tm):
        loads.append(
            pltpu.make_async_remote_copy(
                src_ref=loading_ref, dst_ref=lbuf.at[mt],
                send_sem=lsem_s.at[k], recv_sem=lsem_r.at[k],
                device_id={"tm": lax.rem(mt + k, n_tm)}, device_id_type=MESH,
            )
        )
        loads[-1].start()
    lbuf[mt] = loading_ref[...]

    for u in range(upper):
        size = (offsets[1] if upper > 1 else slots) if u == 0 else SMALL
        member = ids_ref[u : u + 1, :] - ids_ref[u : u + 1, 0:1]
        for at in range(0, size, SMALL * 2 if size % (SMALL * 2) == 0 else SMALL):
            rows = min(SMALL * 2, size)
            slot = lax.broadcasted_iota(jnp.int32, (rows, count), 0) + at
            hot[offsets[u] + at : offsets[u] + at + rows, :] = jnp.where(
                slot == member, 1.0, 0.0
            ).astype(BF16)

    residual = target_ref[...] - location_ref[...]
    variance = variance_ref[...]
    for t in range(steps):
        base = t * wide + rank
        v[base : base + 16, :] = jnp.zeros((16, count), F32)
        v[base : base + steps, :] = variance
        v[base + steps : base + 2 * steps, :] = residual
    aux = v[rank : rank + 8, :]
    one = aux.astype(BF16).astype(F32)
    two = (aux - one).astype(BF16).astype(F32)
    three = aux - one - two
    head = (steps + 1) * rank
    x[head : head + 32, :] = jnp.concatenate([one, two, three, jnp.zeros_like(one)], axis=0).astype(BF16)
    for t in range(steps):
        x[t * rank : (t + 1) * rank, :] = drift_ref[t]

    for copy in loads:
        copy.wait_recv()
    for j in range(n_tm):
        x[steps * rank : head, j * part : (j + 1) * part] = lbuf[j]
    loading = x[steps * rank : head, :].astype(F32)
    for t in range(steps):
        v[t * wide : t * wide + rank, :] = loading + drift_ref[t].astype(F32)

    sums = bdot(x[...], hot[...], NT)
    for t in range(steps):
        z[t * wide : t * wide + rank, :] = sums[t * rank : (t + 1) * rank] + sums[steps * rank : head]
        base = t * wide + rank
        z[base : base + 8, :] = (
            sums[head : head + 8] + sums[head + 8 : head + 16] + sums[head + 16 : head + 24]
        )
        z[base + 8 : base + 16, :] = jnp.zeros((8, slots), F32)

    row8 = lax.broadcasted_iota(jnp.int32, (8, slots), 0)
    slot8 = lax.broadcasted_iota(jnp.int32, (8, slots), 1)
    pick = jnp.zeros((8, slots), F32)
    put = jnp.zeros((8, slots), F32)
    col_row = lax.broadcasted_iota(jnp.int32, (8, 1), 0)
    ids_sent = jnp.full((8, 1), -1.0, F32)
    ids_mine = jnp.full((8, 1), -2.0, F32)
    for u in range(upper):
        first = ids_ref[u : u + 1, 0:1]
        last = ids_ref[u : u + 1, count - 1 : count]
        final = last - first + offsets[u]
        at_first = jnp.where(slot8 == offsets[u], 1.0, 0.0)
        at_last = jnp.where(slot8 == final, 1.0, 0.0)
        pick = jnp.where(row8 == u, at_first, jnp.where(row8 == u + upper, at_last, pick))
        put = jnp.where(row8 == u, at_last, jnp.where(row8 == u + upper, at_first, put))
        first = first.astype(F32)
        last = last.astype(F32)
        ids_sent = jnp.where(col_row == u, first, jnp.where(col_row == u + upper, last, ids_sent))
        ids_mine = jnp.where(col_row == u, last, jnp.where(col_row == u + upper, first, ids_mine))
    lane_p = lax.broadcasted_iota(jnp.int32, (8, steps * wide), 1)
    id_lane = rank + 8
    bnd[me] = jnp.where(lane_p == id_lane, ids_sent, exact(pick, z[...], NT))

    def bnd_copy(k):
        return pltpu.make_async_remote_copy(
            src_ref=bnd.at[me], dst_ref=bnd.at[me], send_sem=bsem_s, recv_sem=bsem_r,
            device_id={"series": lax.rem(me + k, n_series)}, device_id_type=MESH,
        )

    def bnd_start(k, c):
        bnd_copy(k).start()
        return c

    lax.fori_loop(1, n_series, bnd_start, 0)

    def send_matrix(m, value):
        @pl.when(me == m)
        def _():
            crecv[me] = value

        @pl.when(me != m)
        def _():
            cs[m] = value
            pltpu.make_async_remote_copy(
                src_ref=cs.at[m], dst_ref=crecv.at[me], send_sem=csem_s, recv_sem=csem_r,
                device_id={"series": jnp.int32(m)}, device_id_type=MESH,
            ).start()

    for t in range(steps):
        full = v[t * wide : (t + 1) * wide, :]
        weights = 1.0 / variance[t : t + 1]
        send_matrix(t, dot3(split(full[:rank] * weights), split(full), NT))

    many = pltpu.make_async_copy(
        bnd.at[pl.ds(0, n_series - 1)], bnd.at[pl.ds(0, n_series - 1)], bsem_r
    )
    many.wait()

    def join(d, carry):
        total, gate = carry
        theirs = bnd[d]
        higher = jnp.where(d > me, 1.0, 0.0)
        lower = jnp.where(d < me, 1.0, 0.0)
        same = jnp.where(theirs[:, id_lane : id_lane + 1] == ids_mine, 1.0, 0.0)
        mask = same * jnp.where(col_row < upper, higher, lower)
        return total + mask * theirs, jnp.maximum(gate, mask)

    total, gate = lax.fori_loop(
        0, n_series, join, (jnp.zeros((8, steps * wide), F32), jnp.zeros((8, 1), F32))
    )
    total = jnp.where(lane_p == id_lane, 0.0, total)
    z[...] = z[...] + exact(total, put, TN)
    owned = 1.0 - jnp.sum(put * jnp.where(col_row < upper, gate, 0.0), axis=0, keepdims=True)

    slot1 = lax.broadcasted_iota(jnp.int32, (1, slots), 1)
    level_of = jnp.zeros((1, slots), jnp.int32)
    for u in range(1, upper):
        level_of = jnp.where(slot1 >= offsets[u], u, level_of)
    tail = slots - 128
    node_weights = []
    for t in range(steps):
        full = z[t * wide : (t + 1) * wide, :]
        var = full[rank + t : rank + t + 1]
        weights = 1.0 / jnp.where(var > 0.0, var, 1.0)
        node_weights.append(weights)
        scaled = full[:rank] * (weights * owned)
        right = split(full)
        send_matrix(steps + t, dot3(split(jnp.where(level_of == 0, scaled, 0.0)), right, NT))
        end = (right[0][:, tail:], right[1][:, tail:])
        for u in range(1, upper):
            left = jnp.where(level_of[:, tail:] == u, scaled[:, tail:], 0.0)
            send_matrix((u + 1) * steps + t, dot3(split(left), end, NT))

    def inv_copy(k):
        return pltpu.make_async_remote_copy(
            src_ref=invs.at[me], dst_ref=invs.at[me], send_sem=isem_s, recv_sem=isem_r,
            device_id={"series": lax.rem(me + k, n_series)}, device_id_type=MESH,
        )

    def solve():
        pltpu.make_async_copy(
            crecv.at[pl.ds(0, n_series - 1)], crecv.at[pl.ds(0, n_series - 1)], csem_r
        ).wait()
        shape = (rank, wide)
        eye = jnp.where(
            lax.broadcasted_iota(jnp.int32, shape, 0) == lax.broadcasted_iota(jnp.int32, shape, 1), 1.0, 0.0
        )
        a = lax.fori_loop(0, n_series, lambda d, c: c + crecv[d], eye)
        invs[me] = invert(a, rank)

        def start(k, c):
            inv_copy(k).start()
            return c

        lax.fori_loop(1, n_series, start, 0)
        pltpu.make_async_copy(
            invs.at[pl.ds(0, mats - 1)], invs.at[pl.ds(0, mats - 1)], isem_r
        ).wait()

    if n_series == mats:
        solve()
    else:
        pl.when(me < mats)(solve)

        @pl.when(me >= mats)
        def _():
            pltpu.make_async_copy(invs, invs, isem_r).wait()

    g[...] = jnp.zeros_like(g)
    for t in range(steps):
        full = z[t * wide : (t + 1) * wide, :]
        vec = full[:rank]
        weights = node_weights[t]
        res = full[rank + steps + t : rank + steps + t + 1]
        c = rank + steps + t
        parts = split(vec)
        end = (parts[0][:, tail:], parts[1][:, tail:])
        first = invs[steps + t]
        solved = dot3(split(first[:, :rank]), parts, NN)
        solved_end = solved[:, tail:]
        coef = jnp.broadcast_to(first[:, c : c + 1], (rank, slots))
        scale = jnp.broadcast_to(weight_ref[1:2, t : t + 1], (1, slots))
        for u in range(1, upper):
            inv = invs[(u + 1) * steps + t]
            here = level_of[:, tail:] == u
            solved_end = jnp.where(here, dot3(split(inv[:, :rank]), end, NN), solved_end)
            coef = jnp.where(level_of == u, inv[:, c : c + 1], coef)
            scale = jnp.where(level_of == u, weight_ref[u + 1 : u + 2, t : t + 1], scale)
        solved = jnp.concatenate([solved[:, :tail], solved_end], axis=1)
        fitted = jnp.sum(vec * coef, axis=0, keepdims=True)
        white = weights * (res - fitted)
        leverage = jnp.sum(vec * solved, axis=0, keepdims=True)
        base = steps * rank
        g[t * rank : (t + 1) * rank, :] = scale * (solved * weights - coef * white)
        g[base + t : base + t + 1, :] = -scale * white
        g[base + steps + t : base + steps + t + 1, :] = (
            scale * 0.5 * (weights - weights * weights * leverage - white * white)
        )
    ghi, glo = split(g[...])
    height = g.shape[0]
    gs[:height, :] = ghi
    gs[height:, :] = glo

    inv_parts = [split(invs[t][:, :rank]) for t in range(steps)]
    copies = []
    for k in list(range(1, n_tm)) + [0]:
        j = lax.rem(mt + k, n_tm)
        cols = pl.ds(pl.multiple_of(j * part, part), part)
        both = bdot(gs[...], hot[:, cols], NN)
        up = both[:height] + both[height:]
        loading_sum = None
        for t in range(steps):
            c = rank + steps + t
            vec = v[t * wide : t * wide + rank, cols]
            var = v[rank + t : rank + t + 1, cols]
            res = v[rank + steps + t : rank + steps + t + 1, cols]
            weights = 1.0 / var
            coef = invs[t][:, c : c + 1]
            scale = weight_ref[0:1, t : t + 1]
            solved = dot3(inv_parts[t], split(vec), NN)
            fitted = jnp.sum(vec * coef, axis=0, keepdims=True)
            white = weights * (res - fitted)
            leverage = jnp.sum(vec * solved, axis=0, keepdims=True)
            base = steps * rank
            drift = up[t * rank : (t + 1) * rank] + scale * (solved * weights - coef * white)
            gdrift_ref[t, :, cols] = drift
            gloc_ref[t : t + 1, cols] = up[base + t : base + t + 1] - scale * white
            gvar_ref[t : t + 1, cols] = up[base + steps + t : base + steps + t + 1] + scale * 0.5 * (
                weights - weights * weights * leverage - white * white
            )
            loading_sum = drift if loading_sum is None else loading_sum + drift
        if k:
            lsend[k] = loading_sum
            copy = pltpu.make_async_remote_copy(
                src_ref=lsend.at[k], dst_ref=lrecv.at[k],
                send_sem=gsem_s.at[k], recv_sem=gsem_r.at[k],
                device_id={"tm": j}, device_id_type=MESH,
            )
            copy.start()
            copies.append(copy)
    for k, copy in zip(range(1, n_tm), copies):
        copy.wait_recv()
        loading_sum = loading_sum + lrecv[k]
    gload_ref[...] = loading_sum

    for copy in loads + copies:
        copy.wait_send()
    pltpu.make_async_copy(
        bnd.at[pl.ds(0, n_series - 1)], bnd.at[pl.ds(0, n_series - 1)], bsem_s
    ).wait()

    def sent(own):
        held = cs.at[pl.ds(0, mats - 1 if own else mats)]
        pltpu.make_async_copy(held, held, csem_s).wait()
        if own:
            pltpu.make_async_copy(
                crecv.at[pl.ds(0, n_series - 1)], crecv.at[pl.ds(0, n_series - 1)], isem_s
            ).wait()

    if n_series == mats:
        sent(True)
    else:
        pl.when(me < mats)(functools.partial(sent, True))
        pl.when(me >= mats)(functools.partial(sent, False))


def local(target, location, variance, factor_drift, loading, node_ids, level_weight):
    steps, rank, count = factor_drift.shape
    upper = node_ids.shape[0]
    n_series, n_tm = lax.axis_size("series"), lax.axis_size("tm")
    slots = count // 4
    part = count // n_tm
    wide = rank + 16
    mats = (upper + 1) * steps
    height = steps * rank + 16
    vmem = pl.BlockSpec(memory_space=pltpu.VMEM)
    dma = pltpu.SemaphoreType.DMA
    return pl.pallas_call(
        functools.partial(kernel, n_series, n_tm),
        out_shape=(
            jax.ShapeDtypeStruct((steps, count), F32),
            jax.ShapeDtypeStruct((steps, count), F32),
            jax.ShapeDtypeStruct((steps, rank, count), F32),
            jax.ShapeDtypeStruct((rank, part), F32),
        ),
        in_specs=[vmem] * 7,
        out_specs=(vmem,) * 4,
        scratch_shapes=[
            pltpu.VMEM((n_tm, rank, part), BF16),
            pltpu.VMEM(((steps + 1) * rank + 32, count), BF16),
            pltpu.VMEM((slots, count), BF16),
            pltpu.VMEM((steps * wide, count), F32),
            pltpu.VMEM((steps * wide, slots), F32),
            pltpu.VMEM((n_series, 8, steps * wide), F32),
            pltpu.VMEM((mats, rank, wide), F32),
            pltpu.VMEM((n_series, rank, wide), F32),
            pltpu.VMEM((mats, rank, wide), F32),
            pltpu.VMEM((height, slots), F32),
            pltpu.VMEM((2 * height, slots), BF16),
            pltpu.VMEM((n_tm, rank, part), F32),
            pltpu.VMEM((n_tm, rank, part), F32),
            dma((n_tm,)), dma((n_tm,)),
            dma, dma, dma, dma, dma, dma,
            dma((n_tm,)), dma((n_tm,)),
        ],
        compiler_params=pltpu.CompilerParams(
            collective_id=0, has_side_effects=True, vmem_limit_bytes=48 * 1024 * 1024
        ),
    )(target, location, variance, factor_drift, loading, node_ids, level_weight)


def solution(mesh):
    return jax.shard_map(
        local,
        mesh=mesh,
        in_specs=(
            P("tm", "series"),
            P("tm", "series"),
            P("tm", "series"),
            P("tm", None, "series"),
            P(None, ("series", "tm")),
            P(None, "series"),
            P(None, "tm"),
        ),
        out_specs=(
            P("tm", "series"),
            P("tm", "series"),
            P("tm", None, "series"),
            P(None, ("series", "tm")),
        ),
        check_vma=False,
    )
```

time: 501 us -> 51.4 us (0.10)
  other arithmetic: 161 us -> 0 us
  blocking collectives: 155 us -> 0 us
  local copies, waits for them, and re-layouts: 85.6 us -> 8.39 us
  waiting for transfers between devices: 65.5 us -> 0 us
  Pallas kernels: 0 us -> 41.4 us
  between operations: 21.3 us -> 0.65 us
  matrix products: 11.3 us -> 0 us
    all_gather x7 -> x0, blocking collectives: 113 us -> none  [the longest x6 105 us: entering(): everything = jax.tree.map(lambda part: lax.all_gather(part, axis), value)]
    another operation x33 -> x0, other arithmetic: 99.4 us -> none  [the longest x10 47.4 us: level_solve(): lower_factors = jnp.linalg.cholesky(capacitance)]
    gather x18 -> x0, local copies, waits for them, and re-layouts: 72.8 us -> none  [the longest x6 27.8 us: local(): jnp.take(node_factor, member_ids, axis=2)]
    psum x1 -> x0, waiting for transfers between devices: 61.2 us -> none  [local(): upper_cap, upper_proj = lax.psum((upper_cap, upper_proj), 'series')]
    scatter-add x3 -> x0, other arithmetic: 45.7 us -> none  [level_nodes(): jax.ops.segment_sum(packed, member_ids, num_segments=slot_total, indices_...]
    pallas_call x0 -> x1, Pallas kernels: none -> 41.4 us  [local(): pl.pallas_call(functools.partial(kernel, n_series, n_tm), out_shape=(jax....]
    psum x1 -> x0, blocking collectives: 27 us -> none  [local(): bottom_cap, bottom_proj = lax.psum((bottom_cap, bottom_proj), 'series')]
    unnamed x1 -> x0, blocking collectives: 15.1 us -> none
  transfers between devices with their start and end apart: 2 -> 0, of which waited for: 2 -> 0; matrix products, arithmetic and copies ran while one was open for 5% -> 0% of each run, Pallas kernels for 0% -> 0%
where the time goes in v1:
time: 51.4 us; the launch traced here: 50.4 us
  Pallas kernels  41.4 us (81%)
  local copies, waits for them, and re-layouts  8.39 us (16%)
  between operations  0.65 us (1%)
    pallas_call x1, Pallas kernels, local(): pl.pallas_call(functools.partial(kernel, n_series, n_tm), out_shape=(jax....  41.4 us
    unnamed x17, local copies, waits for them, and re-layouts  8.39 us

profile of v1, /device:TPU:1, one launch (start us, length us, event | category | flops | bytes accessed | tf_op | source)
XLA Modules:
  0.0 50.4 jit_solution(1008288875503875167)
XLA Ops:
  0.6 0.8 %copy.11.weight_ref = f32[4,2]{1,0:T(4,128)S(1)} copy(f32[4,2]{0,1:T(2,128)} %param.13) | data formatting | bytes 64 | tf_op args[6]
  1.4 0.0 copy-start
  1.4 1.0 %copy-done = bf16[2,64,2048]{2,1,0:T(8,128)(2,1)S(1)} copy-done((bf16[2,64,2048]{2,1,0:T(8,128)(2,1)S(1)}, bf16[2,64,2048]{2,1,0:T(8,128)(2,1)}, u32[]{:S(2)}) %copy-start) | copy-done | bytes 524312
  2.4 0.0 copy-start.1
  2.4 0.8 %copy-done.1 = bf16[64,512]{1,0:T(8,128)(2,1)S(1)} copy-done((bf16[64,512]{1,0:T(8,128)(2,1)S(1)}, bf16[64,512]{1,0:T(8,128)(2,1)}, u32[]{:S(2)}) %copy-start.1) | copy-done | bytes 65560
  3.3 0.0 copy-start.2
  3.3 0.8 %copy-done.2 = s32[3,2048]{1,0:T(4,128)S(1)} copy-done((s32[3,2048]{1,0:T(4,128)S(1)}, s32[3,2048]{1,0:T(4,128)}, u32[]{:S(2)}) %copy-start.2) | copy-done | bytes 24600
  4.0 0.0 copy-start.3
  4.0 0.7 %copy-done.3 = f32[2,2048]{1,0:T(2,128)S(1)} copy-done((f32[2,2048]{1,0:T(2,128)S(1)}, f32[2,2048]{1,0:T(2,128)}, u32[]{:S(2)}) %copy-start.3) | copy-done | bytes 16408
  4.8 0.0 copy-start.4
  4.8 0.7 %copy-done.4 = f32[2,2048]{1,0:T(2,128)S(1)} copy-done((f32[2,2048]{1,0:T(2,128)S(1)}, f32[2,2048]{1,0:T(2,128)}, u32[]{:S(2)}) %copy-start.4) | copy-done | bytes 16408
  5.5 0.0 copy-start.5
  5.5 0.7 %copy-done.5 = f32[2,2048]{1,0:T(2,128)S(1)} copy-done((f32[2,2048]{1,0:T(2,128)S(1)}, f32[2,2048]{1,0:T(2,128)}, u32[]{:S(2)}) %copy-start.5) | copy-done | bytes 16408
  6.2 41.4 %shard_map.102 = (f32[2,2048]{1,0:T(2,128)S(1)}, f32[2,2048]{1,0:T(2,128)S(1)}, f32[2,64,2048]{2,1,0:T(8,128)S(1)}, f32[64,512]{1,0:T(8,128)S(1)}) custom-call(f32[2,2048]{1,0:T(2,128)S(1)} %copy-done.3, f32[2,2048]{1,0:T(2,128)S(1)} %copy-done.4, f32[2,2048]{1,0:T(2,128)S(1)} %copy-done.5, bf16[2,64,2048]{2,1,0:T(8,128)(2,1)S(1)} %copy-done, ...), custom_call_target="tpu_custom_call" | custom-call | tf_op jit(solution)/shard_map/pallas_call | solution.py:377
  47.6 0.6 %copy.16 = f32[2,2048]{1,0:T(2,128)} copy(f32[2,2048]{1,0:T(2,128)S(1)} %get-tuple-element.8) | data formatting | bytes 32768
  48.2 0.6 %copy.17 = f32[2,2048]{1,0:T(2,128)} copy(f32[2,2048]{1,0:T(2,128)S(1)} %get-tuple-element.9) | data formatting | bytes 32768
  48.8 1.0 %copy.18 = f32[2,64,2048]{2,1,0:T(8,128)} copy(f32[2,64,2048]{2,1,0:T(8,128)S(1)} %get-tuple-element.10) | data formatting | bytes 2097152
  49.8 0.7 %copy.19 = f32[64,512]{1,0:T(8,128)} copy(f32[64,512]{1,0:T(8,128)S(1)} %get-tuple-element.11) | data formatting | bytes 262144
Async XLA Ops:
  1.4 1.0 %copy-start = (bf16[2,64,2048]{2,1,0:T(8,128)(2,1)S(1)}, bf16[2,64,2048]{2,1,0:T(8,128)(2,1)}, u32[]{:S(2)}) copy-start(bf16[2,64,2048]{2,1,0:T(8,128)(2,1)} %drift_ref.1) | copy-start | bytes 1572868
  2.4 0.8 %copy-start.1 = (bf16[64,512]{1,0:T(8,128)(2,1)S(1)}, bf16[64,512]{1,0:T(8,128)(2,1)}, u32[]{:S(2)}) copy-start(bf16[64,512]{1,0:T(8,128)(2,1)} %loading_ref.1) | copy-start | bytes 196612
  3.3 0.8 %copy-start.2 = (s32[3,2048]{1,0:T(4,128)S(1)}, s32[3,2048]{1,0:T(4,128)}, u32[]{:S(2)}) copy-start(s32[3,2048]{1,0:T(4,128)} %ids_ref.1) | copy-start | bytes 73732
  4.0 0.7 %copy-start.3 = (f32[2,2048]{1,0:T(2,128)S(1)}, f32[2,2048]{1,0:T(2,128)}, u32[]{:S(2)}) copy-start(f32[2,2048]{1,0:T(2,128)} %target_ref.1) | copy-start | bytes 49156
  4.8 0.7 %copy-start.4 = (f32[2,2048]{1,0:T(2,128)S(1)}, f32[2,2048]{1,0:T(2,128)}, u32[]{:S(2)}) copy-start(f32[2,2048]{1,0:T(2,128)} %location_ref.1) | copy-start | bytes 49156
  5.5 0.7 %copy-start.5 = (f32[2,2048]{1,0:T(2,128)S(1)}, f32[2,2048]{1,0:T(2,128)}, u32[]{:S(2)}) copy-start(f32[2,2048]{1,0:T(2,128)} %variance_ref.1) | copy-start | bytes 49156

commit v2 on v1

--- a/solution.py
+++ b/solution.py
@@ -35,6 +35,19 @@
     return lax.dot_general(
         a, b, dims, precision=lax.Precision.HIGHEST, preferred_element_type=F32
     )
+
+
+def pack(value, rank):
+    half = rank // 2
+    left = jnp.concatenate([value[:half, :rank], value[rank : rank + 8, :rank]], axis=0)
+    right = jnp.concatenate([value[half:rank, :rank], jnp.zeros((8, rank), F32)], axis=0)
+    return jnp.concatenate([left, right], axis=1)
+
+
+def unpack(packed):
+    half, rank = packed.shape[0] - 8, packed.shape[1] // 2
+    matrix = jnp.concatenate([packed[:half, :rank], packed[:half, rank:]], axis=0)
+    return matrix, packed[half:]
 
 
 def invert(a, size):
@@ -52,13 +65,14 @@
 
 def kernel(
     n_series, n_tm,
-    target_ref, location_ref, variance_ref, drift_ref, loading_ref, ids_ref, weight_ref,
+    target_hbm, location_hbm, variance_hbm, drift_hbm, loading_hbm, ids_hbm, weight_hbm,
     gloc_ref, gvar_ref, gdrift_ref, gload_ref,
+    target_ref, location_ref, variance_ref, drift_ref, loading_ref, ids_ref, weight_ref, in_sem,
     lbuf, x, hot, v, z, bnd, cs, crecv, invs, g, gs, lsend, lrecv,
     lsem_s, lsem_r, bsem_s, bsem_r, csem_s, csem_r, isem_s, isem_r, gsem_s, gsem_r,
 ):
-    steps, rank, count = drift_ref.shape
-    upper = ids_ref.shape[0]
+    steps, rank, count = drift_hbm.shape
+    upper = ids_hbm.shape[0]
     slots = hot.shape[0]
     wide = rank + 16
     mats = (upper + 1) * steps
@@ -68,6 +82,16 @@
     mt = lax.axis_index("tm")
 
     barrier = pltpu.get_barrier_semaphore()
+    ins = [
+        pltpu.make_async_copy(src, dst, in_sem.at[i])
+        for i, (src, dst) in enumerate((
+            (loading_hbm, loading_ref), (ids_hbm, ids_ref), (target_hbm, target_ref),
+            (location_hbm, location_ref), (variance_hbm, variance_ref),
+            (drift_hbm, drift_ref), (weight_hbm, weight_ref),
+        ))
+    ]
+    for copy in ins:
+        copy.start()
 
     def hello(k, c):
         pl.semaphore_signal(
@@ -83,6 +107,7 @@
     pl.semaphore_wait(barrier, n_series - 1 + n_tm - 1)
 
     loads = []
+    ins[0].wait()
     for k in range(1, n_tm):
         loads.append(
             pltpu.make_async_remote_copy(
@@ -94,6 +119,7 @@
         loads[-1].start()
     lbuf[mt] = loading_ref[...]
 
+    ins[1].wait()
     for u in range(upper):
         size = (offsets[1] if upper > 1 else slots) if u == 0 else SMALL
         member = ids_ref[u : u + 1, :] - ids_ref[u : u + 1, 0:1]
@@ -104,6 +130,8 @@
                 slot == member, 1.0, 0.0
             ).astype(BF16)
 
+    for copy in ins[2:]:
+        copy.wait()
     residual = target_ref[...] - location_ref[...]
     variance = variance_ref[...]
     for t in range(steps):
@@ -172,7 +200,9 @@
 
     lax.fori_loop(1, n_series, bnd_start, 0)
 
-    def send_matrix(m, value):
+    def send_matrix(m, whole):
+        value = pack(whole, rank)
+
         @pl.when(me == m)
         def _():
             crecv[me] = value
@@ -188,7 +218,7 @@
     for t in range(steps):
         full = v[t * wide : (t + 1) * wide, :]
         weights = 1.0 / variance[t : t + 1]
-        send_matrix(t, dot3(split(full[:rank] * weights), split(full), NT))
+        send_matrix(t, dot3(split(full * weights), split(full), NT))
 
     many = pltpu.make_async_copy(
         bnd.at[pl.ds(0, n_series - 1)], bnd.at[pl.ds(0, n_series - 1)], bsem_r
@@ -222,7 +252,7 @@
         var = full[rank + t : rank + t + 1]
         weights = 1.0 / jnp.where(var > 0.0, var, 1.0)
         node_weights.append(weights)
-        scaled = full[:rank] * (weights * owned)
+        scaled = full * (weights * owned)
         right = split(full)
         send_matrix(steps + t, dot3(split(jnp.where(level_of == 0, scaled, 0.0)), right, NT))
         end = (right[0][:, tail:], right[1][:, tail:])
@@ -240,12 +270,13 @@
         pltpu.make_async_copy(
             crecv.at[pl.ds(0, n_series - 1)], crecv.at[pl.ds(0, n_series - 1)], csem_r
         ).wait()
-        shape = (rank, wide)
+        shape = (rank, rank)
         eye = jnp.where(
             lax.broadcasted_iota(jnp.int32, shape, 0) == lax.broadcasted_iota(jnp.int32, shape, 1), 1.0, 0.0
         )
-        a = lax.fori_loop(0, n_series, lambda d, c: c + crecv[d], eye)
-        invs[me] = invert(a, rank)
+        a, below = unpack(lax.fori_loop(1, n_series, lambda d, c: c + crecv[d], crecv[0]))
+        a = invert(a + eye, rank)
+        invs[me] = pack(jnp.concatenate([a, exact(below[:, :rank], a, NN)], axis=0), rank)
 
         def start(k, c):
             inv_copy(k).start()
@@ -265,26 +296,31 @@
         def _():
             pltpu.make_async_copy(invs, invs, isem_r).wait()
 
+    inverses, coefs = [], []
+    for m in range(mats):
+        matrix, below = unpack(invs[m])
+        inverses.append(split(matrix))
+        c = steps + m % steps
+        coefs.append(below.T[:rank, c : c + 1])
+
     g[...] = jnp.zeros_like(g)
     for t in range(steps):
         full = z[t * wide : (t + 1) * wide, :]
         vec = full[:rank]
         weights = node_weights[t]
         res = full[rank + steps + t : rank + steps + t + 1]
-        c = rank + steps + t
         parts = split(vec)
         end = (parts[0][:, tail:], parts[1][:, tail:])
-        first = invs[steps + t]
-        solved = dot3(split(first[:, :rank]), parts, NN)
+        solved = dot3(inverses[steps + t], parts, NN)
         solved_end = solved[:, tail:]
-        coef = jnp.broadcast_to(first[:, c : c + 1], (rank, slots))
-        scale = jnp.broadcast_to(weight_ref[1:2, t : t + 1], (1, slots))
+        coef = jnp.broadcast_to(coefs[steps + t], (rank, slots))
+        scale = jnp.broadcast_to(weight_ref[t : t + 1, 1:2], (1, slots))
         for u in range(1, upper):
-            inv = invs[(u + 1) * steps + t]
+            m = (u + 1) * steps + t
             here = level_of[:, tail:] == u
-            solved_end = jnp.where(here, dot3(split(inv[:, :rank]), end, NN), solved_end)
-            coef = jnp.where(level_of == u, inv[:, c : c + 1], coef)
-            scale = jnp.where(level_of == u, weight_ref[u + 1 : u + 2, t : t + 1], scale)
+            solved_end = jnp.where(here, dot3(inverses[m], end, NN), solved_end)
+            coef = jnp.where(level_of == u, coefs[m], coef)
+            scale = jnp.where(level_of == u, weight_ref[t : t + 1, u + 1 : u + 2], scale)
         solved = jnp.concatenate([solved[:, :tail], solved_end], axis=1)
         fitted = jnp.sum(vec * coef, axis=0, keepdims=True)
         white = weights * (res - fitted)
@@ -300,7 +336,6 @@
     gs[:height, :] = ghi
     gs[height:, :] = glo
 
-    inv_parts = [split(invs[t][:, :rank]) for t in range(steps)]
     copies = []
     for k in list(range(1, n_tm)) + [0]:
         j = lax.rem(mt + k, n_tm)
@@ -309,14 +344,13 @@
         up = both[:height] + both[height:]
         loading_sum = None
         for t in range(steps):
-            c = rank + steps + t
             vec = v[t * wide : t * wide + rank, cols]
             var = v[rank + t : rank + t + 1, cols]
             res = v[rank + steps + t : rank + steps + t + 1, cols]
             weights = 1.0 / var
-            coef = invs[t][:, c : c + 1]
-            scale = weight_ref[0:1, t : t + 1]
-            solved = dot3(inv_parts[t], split(vec), NN)
+            coef = coefs[t]
+            scale = weight_ref[t : t + 1, 0:1]
+            solved = dot3(inverses[t], split(vec), NN)
             fitted = jnp.sum(vec * coef, axis=0, keepdims=True)
             white = weights * (res - fitted)
             leverage = jnp.sum(vec * solved, axis=0, keepdims=True)
@@ -374,6 +408,8 @@
     height = steps * rank + 16
     vmem = pl.BlockSpec(memory_space=pltpu.VMEM)
     dma = pltpu.SemaphoreType.DMA
+    operands = (target, location, variance, factor_drift, loading, node_ids, level_weight.T)
+    operands = [pltpu.with_memory_space_constraint(a, pltpu.HBM) for a in operands]
     return pl.pallas_call(
         functools.partial(kernel, n_series, n_tm),
         out_shape=(
@@ -382,18 +418,26 @@
             jax.ShapeDtypeStruct((steps, rank, count), F32),
             jax.ShapeDtypeStruct((rank, part), F32),
         ),
-        in_specs=[vmem] * 7,
+        in_specs=[pl.BlockSpec(memory_space=pltpu.HBM)] * 7,
         out_specs=(vmem,) * 4,
         scratch_shapes=[
+            pltpu.VMEM((steps, count), F32),
+            pltpu.VMEM((steps, count), F32),
+            pltpu.VMEM((steps, count), F32),
+            pltpu.VMEM((steps, rank, count), BF16),
+            pltpu.VMEM((rank, part), BF16),
+            pltpu.VMEM((upper, count), jnp.int32),
+            pltpu.VMEM((steps, upper + 1), F32),
+            dma((7,)),
             pltpu.VMEM((n_tm, rank, part), BF16),
             pltpu.VMEM(((steps + 1) * rank + 32, count), BF16),
             pltpu.VMEM((slots, count), BF16),
             pltpu.VMEM((steps * wide, count), F32),
             pltpu.VMEM((steps * wide, slots), F32),
             pltpu.VMEM((n_series, 8, steps * wide), F32),
-            pltpu.VMEM((mats, rank, wide), F32),
-            pltpu.VMEM((n_series, rank, wide), F32),
-            pltpu.VMEM((mats, rank, wide), F32),
+            pltpu.VMEM((mats, rank // 2 + 8, 2 * rank), F32),
+            pltpu.VMEM((n_series, rank // 2 + 8, 2 * rank), F32),
+            pltpu.VMEM((mats, rank // 2 + 8, 2 * rank), F32),
             pltpu.VMEM((height, slots), F32),
             pltpu.VMEM((2 * height, slots), BF16),
             pltpu.VMEM((n_tm, rank, part), F32),
@@ -405,7 +449,7 @@
         compiler_params=pltpu.CompilerParams(
             collective_id=0, has_side_effects=True, vmem_limit_bytes=48 * 1024 * 1024
         ),
-    )(target, location, variance, factor_drift, loading, node_ids, level_weight)
+    )(*operands)
 
 
 def solution(mesh):

time: 51.4 us -> 43.3 us (0.84); the launches traced: 50.4 us -> 43.1 us
  local copies, waits for them, and re-layouts: 8.39 us -> 2.84 us
  Pallas kernels: 41.4 us -> 39.7 us
    unnamed x17 -> x4, local copies, waits for them, and re-layouts: 8.39 us -> 2.84 us
    pallas_call x1, Pallas kernels: 41.4 us -> 39.7 us  [local(): pl.pallas_call(functools.partial(kernel, n_series, n_tm), out_shape=(jax....]
where the time goes in v2:
time: 43.3 us; the launch traced here: 43.1 us
  Pallas kernels  39.7 us (92%)
  local copies, waits for them, and re-layouts  2.84 us (7%)
  between operations  0.64 us (1%)
    pallas_call x1, Pallas kernels, local(): pl.pallas_call(functools.partial(kernel, n_series, n_tm), out_shape=(jax....  39.7 us
    unnamed x4, local copies, waits for them, and re-layouts  2.84 us

profile of v2, /device:TPU:1, one launch (start us, length us, event | category | flops | bytes accessed | tf_op | source)
XLA Modules:
  0.0 43.1 jit_solution(343679260185817095)
XLA Ops:
  0.6 39.7 %shard_map.102 = (f32[2,2048]{1,0:T(2,128)S(1)}, f32[2,2048]{1,0:T(2,128)S(1)}, f32[2,64,2048]{2,1,0:T(8,128)S(1)}, f32[64,512]{1,0:T(8,128)S(1)}) custom-call(f32[2,2048]{1,0:T(2,128)} %target_hbm.1, f32[2,2048]{1,0:T(2,128)} %location_hbm.1, f32[2,2048]{1,0:T(2,128)} %variance_hbm.1, bf16[2,64,2048]{2,1,0:T(8,128)(2,1)} %drift_hbm.1, ...), custom_call_target="tpu_custom_call" | custom-call | tf_op jit(solution)/shard_map/pallas_call | solution.py:413
  40.3 0.6 %copy.15 = f32[2,2048]{1,0:T(2,128)} copy(f32[2,2048]{1,0:T(2,128)S(1)} %get-tuple-element.8) | data formatting | bytes 32768
  40.9 0.6 %copy.16 = f32[2,2048]{1,0:T(2,128)} copy(f32[2,2048]{1,0:T(2,128)S(1)} %get-tuple-element.9) | data formatting | bytes 32768
  41.5 1.0 %copy.17 = f32[2,64,2048]{2,1,0:T(8,128)} copy(f32[2,64,2048]{2,1,0:T(8,128)S(1)} %get-tuple-element.10) | data formatting | bytes 2097152
  42.5 0.7 %copy.18 = f32[64,512]{1,0:T(8,128)} copy(f32[64,512]{1,0:T(8,128)S(1)} %get-tuple-element.11) | data formatting | bytes 262144

commit v3 on v2

--- a/solution.py
+++ b/solution.py
@@ -336,9 +336,11 @@
     gs[:height, :] = ghi
     gs[height:, :] = glo
 
-    copies = []
-    for k in list(range(1, n_tm)) + [0]:
-        j = lax.rem(mt + k, n_tm)
+    pairs = n_tm // 2
+    pair, side = mt // 2, lax.rem(mt, 2)
+    sibling = pair * 2 + 1 - side
+
+    def columns(j):
         cols = pl.ds(pl.multiple_of(j * part, part), part)
         both = bdot(gs[...], hot[:, cols], NN)
         up = both[:height] + both[height:]
@@ -362,18 +364,33 @@
                 weights - weights * weights * leverage - white * white
             )
             loading_sum = drift if loading_sum is None else loading_sum + drift
-        if k:
-            lsend[k] = loading_sum
-            copy = pltpu.make_async_remote_copy(
-                src_ref=lsend.at[k], dst_ref=lrecv.at[k],
-                send_sem=gsem_s.at[k], recv_sem=gsem_r.at[k],
-                device_id={"tm": j}, device_id_type=MESH,
-            )
-            copy.start()
-            copies.append(copy)
-    for k, copy in zip(range(1, n_tm), copies):
-        copy.wait_recv()
-        loading_sum = loading_sum + lrecv[k]
+        return loading_sum
+
+    def send(slot, value, to):
+        lsend[slot] = value
+        copy = pltpu.make_async_remote_copy(
+            src_ref=lsend.at[slot], dst_ref=lrecv.at[slot],
+            send_sem=gsem_s.at[slot], recv_sem=gsem_r.at[slot],
+            device_id={"tm": to}, device_id_type=MESH,
+        )
+        copy.start()
+        return copy
+
+    copies = []
+    for q in range(1, pairs):
+        there = lax.rem(pair + q, pairs) * 2
+        near = send(2 * q - 2, columns(there + 1 - side), sibling)
+        both_sum = columns(there + side)
+        near.wait_recv()
+        copies += [near, send(2 * q - 1, both_sum + lrecv[2 * q - 2], there + side)]
+    near = send(2 * pairs - 2, columns(sibling), sibling)
+    loading_sum = columns(mt)
+    near.wait_recv()
+    loading_sum = loading_sum + lrecv[2 * pairs - 2]
+    for q in range(1, pairs):
+        copies[2 * q - 1].wait_recv()
+        loading_sum = loading_sum + lrecv[2 * q - 1]
+    copies.append(near)
     gload_ref[...] = loading_sum
 
     for copy in loads + copies:

time: 43.3 us -> 43.6 us (level)
  no operation moved by 1% of the time
where the time goes in v3:
time: 43.6 us; the launch traced here: 43.1 us
  Pallas kernels  39.7 us (91%)
  local copies, waits for them, and re-layouts  2.84 us (7%)
  between operations  0.64 us (1%)
    pallas_call x1, Pallas kernels, local(): pl.pallas_call(functools.partial(kernel, n_series, n_tm), out_shape=(jax....  39.7 us
    unnamed x4, local copies, waits for them, and re-layouts  2.84 us

profile of v3, /device:TPU:1, one launch (start us, length us, event | category | flops | bytes accessed | tf_op | source)
XLA Modules:
  0.0 43.1 jit_solution(8817968873554203357)
XLA Ops:
  0.6 39.7 %shard_map.102 = (f32[2,2048]{1,0:T(2,128)S(1)}, f32[2,2048]{1,0:T(2,128)S(1)}, f32[2,64,2048]{2,1,0:T(8,128)S(1)}, f32[64,512]{1,0:T(8,128)S(1)}) custom-call(f32[2,2048]{1,0:T(2,128)} %target_hbm.1, f32[2,2048]{1,0:T(2,128)} %location_hbm.1, f32[2,2048]{1,0:T(2,128)} %variance_hbm.1, bf16[2,64,2048]{2,1,0:T(8,128)(2,1)} %drift_hbm.1, ...), custom_call_target="tpu_custom_call" | custom-call | tf_op jit(solution)/shard_map/pallas_call | solution.py:430
  40.3 0.6 %copy.15 = f32[2,2048]{1,0:T(2,128)} copy(f32[2,2048]{1,0:T(2,128)S(1)} %get-tuple-element.8) | data formatting | bytes 32768
  40.9 0.6 %copy.16 = f32[2,2048]{1,0:T(2,128)} copy(f32[2,2048]{1,0:T(2,128)S(1)} %get-tuple-element.9) | data formatting | bytes 32768
  41.5 1.0 %copy.17 = f32[2,64,2048]{2,1,0:T(8,128)} copy(f32[2,64,2048]{2,1,0:T(8,128)S(1)} %get-tuple-element.10) | data formatting | bytes 2097152
  42.5 0.7 %copy.18 = f32[64,512]{1,0:T(8,128)} copy(f32[64,512]{1,0:T(8,128)S(1)} %get-tuple-element.11) | data formatting | bytes 262144

commit v4 on v2

--- a/solution.py
+++ b/solution.py
@@ -254,11 +254,25 @@
         node_weights.append(weights)
         scaled = full * (weights * owned)
         right = split(full)
-        send_matrix(steps + t, dot3(split(jnp.where(level_of == 0, scaled, 0.0)), right, NT))
+        cs[steps + t] = pack(dot3(split(jnp.where(level_of == 0, scaled, 0.0)), right, NT), rank)
         end = (right[0][:, tail:], right[1][:, tail:])
         for u in range(1, upper):
             left = jnp.where(level_of[:, tail:] == u, scaled[:, tail:], 0.0)
-            send_matrix((u + 1) * steps + t, dot3(split(left), end, NT))
+            cs[(u + 1) * steps + t] = pack(dot3(split(left), end, NT), rank)
+
+    for k in range(1, mats - steps + 1):
+        m = steps + lax.rem(me + k, mats - steps)
+
+        @pl.when(me == m)
+        def _():
+            crecv[me] = cs[m]
+
+        @pl.when(me != m)
+        def _():
+            pltpu.make_async_remote_copy(
+                src_ref=cs.at[m], dst_ref=crecv.at[me], send_sem=csem_s, recv_sem=csem_r,
+                device_id={"series": m}, device_id_type=MESH,
+            ).start()
 
     def inv_copy(k):
         return pltpu.make_async_remote_copy(

time: 43.3 us -> 42.7 us (0.986)
  Pallas kernels: 39.7 us -> 39.1 us
    pallas_call x1, Pallas kernels: 39.7 us -> 39.1 us  [local(): pl.pallas_call(functools.partial(kernel, n_series, n_tm), out_shape=(jax....]
where the time goes in v4:
time: 42.7 us; the launch traced here: 42.5 us
  Pallas kernels  39.1 us (92%)
  local copies, waits for them, and re-layouts  2.84 us (7%)
  between operations  0.64 us (1%)
    pallas_call x1, Pallas kernels, local(): pl.pallas_call(functools.partial(kernel, n_series, n_tm), out_shape=(jax....  39.1 us
    unnamed x4, local copies, waits for them, and re-layouts  2.84 us

profile of v4, /device:TPU:1, one launch (start us, length us, event | category | flops | bytes accessed | tf_op | source)
XLA Modules:
  0.0 42.5 jit_solution(13971324324796421814)
XLA Ops:
  0.6 39.1 %shard_map.102 = (f32[2,2048]{1,0:T(2,128)S(1)}, f32[2,2048]{1,0:T(2,128)S(1)}, f32[2,64,2048]{2,1,0:T(8,128)S(1)}, f32[64,512]{1,0:T(8,128)S(1)}) custom-call(f32[2,2048]{1,0:T(2,128)} %target_hbm.1, f32[2,2048]{1,0:T(2,128)} %location_hbm.1, f32[2,2048]{1,0:T(2,128)} %variance_hbm.1, bf16[2,64,2048]{2,1,0:T(8,128)(2,1)} %drift_hbm.1, ...), custom_call_target="tpu_custom_call" | custom-call | tf_op jit(solution)/shard_map/pallas_call | solution.py:427
  39.7 0.6 %copy.15 = f32[2,2048]{1,0:T(2,128)} copy(f32[2,2048]{1,0:T(2,128)S(1)} %get-tuple-element.8) | data formatting | bytes 32768
  40.3 0.6 %copy.16 = f32[2,2048]{1,0:T(2,128)} copy(f32[2,2048]{1,0:T(2,128)S(1)} %get-tuple-element.9) | data formatting | bytes 32768
  40.9 1.0 %copy.17 = f32[2,64,2048]{2,1,0:T(8,128)} copy(f32[2,64,2048]{2,1,0:T(8,128)S(1)} %get-tuple-element.10) | data formatting | bytes 2097152
  41.9 0.7 %copy.18 = f32[64,512]{1,0:T(8,128)} copy(f32[64,512]{1,0:T(8,128)S(1)} %get-tuple-element.11) | data formatting | bytes 262144
